TPU v7x, 256 devices: a whole 4x4x8 slice. The times are simulated.
256 devices in a mesh: group: 8 (over x, core), sub: 32 (over y, z).
Axes of the slice: x: 4, y: 4, z: 8, core: 2. Of those that a mesh axis runs over, the one named last changes fastest.
Arguments:
- resid_iface: float32 [256, 16, 4352], P(('group', 'sub')), may hold values from -6 to 6
- resid_inner: float32 [256, 16, 3072], P(('group', 'sub')), may hold values from -6 to 6
- weights: float32 [256, 4352], P(('group', 'sub')), may hold values from 0.25 to 0.75
- nbr: int32 [256, 32], P(('group', 'sub')), may hold values from 0 to 1, as said below
- own2: int32 [256, 128], P(('group', 'sub')), may hold values from 0 to 2047
- cidx: int32 [256, 8], P(('group', 'sub')), may hold values from 0 to 16
- neumann: bfloat16 [256, 17, 256, 256], P(('group', 'sub'))
- dirichlet: bfloat16 [256, 8, 384, 384], P(('group', 'sub'))
- coupling: bfloat16 [256, 8, 256, 384], P(('group', 'sub')), may hold values from -0.375 to 0.375
- coarse_basis: bfloat16 [256, 4352, 128], P(('group', 'sub')), may hold values from -0.5 to 0.5
- group_basis: float32 [16384, 512], P(('group', 'sub')), may hold values from -0.25 to 0.25
- group_inverse: float32 [16384, 2048], P('group', 'sub'), as said below
- top_inverse: float32 [512, 512], replicated, as said below
Outputs:
- interface_out: float32 [256, 16, 4352], P(('group', 'sub'))
- interior_out: float32 [256, 16, 3072], P(('group', 'sub'))
Inputs may be any that keep to these rules, and one draw needn't show every extreme that they name: Symmetric within each group (nbr[(g, q), j] = nbr[(g, j), q]) with nbr[(g, q), q] = 0. `group_inverse`: each matrix of a group is symmetric. `top_inverse`: symmetric.
All inputs are finite; a program needn't handle non-finite values.
Results may differ from a plain program's by a relative error of at most 0.013.
Values may be sent and summed in bfloat16 or wider, within the bound.
A program may use at most 64 MiB of HBM per device.

v0:
```python
import jax
import jax.numpy as jnp
from jax import lax
from jax.sharding import PartitionSpec as P


def padded_2(cells, sides, width):
    for axis, dim in sides:
        count = lax.axis_size(axis)
        ends = count - 1
        head = lax.slice_in_dim(cells, 0, width, axis=dim)
        tail = lax.slice_in_dim(cells, cells.shape[dim] - width, cells.shape[dim], axis=dim)
        cells = jnp.concatenate(
            [
                lax.ppermute(tail, axis, [(i, (i + 1) % count) for i in range(ends)]),
                cells,
                lax.ppermute(head, axis, [((i + 1) % count, i) for i in range(ends)]),
            ],
            axis=dim,
        )
    return cells


def shards(
    resid_iface,
    resid_inner,
    weights,
    nbr,
    own2,
    cidx,
    neumann,
    dirichlet,
    coupling,
    coarse_basis,
    group_basis,
    group_inverse,
    top_inverse,
):
    highest = lax.Precision.HIGHEST
    nsub = lax.axis_size("sub")
    mine = lax.axis_index("sub")
    rows = resid_iface.shape[1]
    width = resid_iface.shape[2]
    slot_width = width // (nsub + 2)
    block_count = neumann.shape[1]
    block_width = neumann.shape[2]
    inner_count = dirichlet.shape[1]
    inner_width = dirichlet.shape[2]
    group_width = group_inverse.shape[0]
    share = group_inverse.shape[1]
    slot_mask = jnp.concatenate([nbr[0].astype(jnp.float32), jnp.ones((2,), jnp.float32)])
    scale = jnp.repeat(slot_mask, slot_width) * weights[0]
    weighted = (scale[None, :] * resid_iface[0]).astype(jnp.bfloat16)
    local0 = jnp.dot(weighted, coarse_basis[0], preferred_element_type=jnp.float32)
    onehot = (own2[0][:, None] == jnp.arange(group_width, dtype=jnp.int32)[None, :]).astype(
        jnp.float32
    )
    contrib = jnp.dot(local0, onehot, precision=highest)
    level2 = lax.psum(contrib.astype(jnp.bfloat16), "sub").astype(jnp.float32)
    level2_mine = lax.dynamic_slice_in_dim(level2, mine * share, share, 1)
    neumann_part = jnp.einsum(
        "rkb,kbc->rkc",
        weighted.reshape(rows, block_count, block_width),
        neumann[0],
        preferred_element_type=jnp.float32,
    ).reshape(rows, width)
    top_term = jnp.dot(level2_mine, group_basis, precision=highest)
    level3 = lax.psum(top_term, ("group", "sub"))
    coarse3 = jnp.dot(level3, top_inverse, precision=highest)
    lifted = lax.dot_general(coarse3, group_basis, (((1,), (1,)), ((), ())), precision=highest)
    coarse2_mine = jnp.dot(level2, group_inverse, precision=highest) + lifted
    coarse2 = lax.all_gather(coarse2_mine.astype(jnp.bfloat16), "sub", axis=1, tiled=True)
    values = jnp.take(coarse2, own2[0], axis=1)
    spread = lax.dot_general(
        values, coarse_basis[0], (((1,), (1,)), ((), ())), preferred_element_type=jnp.float32
    )
    scaled = scale[None, :] * (neumann_part + spread)
    slots = scaled.reshape(rows, nsub + 2, slot_width)
    received = lax.all_to_all(
        slots[:, :nsub, :].astype(jnp.bfloat16), "sub", split_axis=1, concat_axis=1, tiled=True
    ).astype(jnp.float32)
    padded = padded_2(slots[:, nsub:, :], (("group", 1),), 1)
    lower_face = slots[:, nsub, :] + padded[:, 0, :]
    upper_face = slots[:, nsub + 1, :] + padded[:, 3, :]
    total = jnp.concatenate(
        [slots[:, :nsub, :] + received, lower_face[:, None, :], upper_face[:, None, :]], axis=1
    )
    interface_out = total.reshape(rows, width)
    iface_blocks = interface_out.reshape(rows, block_count, block_width).astype(jnp.bfloat16)
    picked = jnp.take(iface_blocks, cidx[0], axis=1)
    pushed = jnp.einsum("rkb,kbc->rkc", picked, coupling[0], preferred_element_type=jnp.float32)
    inner_rhs = (resid_inner[0].reshape(rows, inner_count, inner_width) - pushed).astype(
        jnp.bfloat16
    )
    interior_out = jnp.einsum(
        "rkb,kbc->rkc", inner_rhs, dirichlet[0], preferred_element_type=jnp.float32
    ).reshape(rows, inner_count * inner_width)
    return (interface_out[None], interior_out[None])


def solution(mesh):
    placed = (
        P(("group", "sub"), None, None),
        P(("group", "sub"), None, None),
        P(("group", "sub"), None),
        P(("group", "sub"), None),
        P(("group", "sub"), None),
        P(("group", "sub"), None),
        P(("group", "sub"), None, None, None),
        P(("group", "sub"), None, None, None),
        P(("group", "sub"), None, None, None),
        P(("group", "sub"), None, None),
        P(("group", "sub"), None),
        P("group", "sub"),
        P(),
    )
    return jax.shard_map(
        shards,
        mesh=mesh,
        in_specs=placed,
        out_specs=(P(("group", "sub"), None, None), P(("group", "sub"), None, None)),
        check_vma=False,
    )
```

profile of v0, /device:TPU:1, one launch (start us, length us, event | category | flops | bytes accessed | tf_op | source)
XLA Modules:
  0.0 318.7 jit_solution(4623421728509135453)
XLA Ops:
  7.3 0.8 convert_bitcast_fusion
  8.1 0.8 fusion.45
  8.9 1.6 fusion.25
  10.5 1.8 convolution_convert_fusion
  12.6 2.0 fusion.7
  14.6 0.7 copy.43
  15.3 136.0 %all-reduce.3.cloned.1.call-done = bf16[16,2048]{1,0:T(8,128)(2,1)} async-done(((bf16[16,2048]{1,0:T(8,128)(2,1)}), bf16[16,2048]{1,0:T(8,128)(2,1)}) %all-reduce.3.cloned.1.call-update) | async-done | bytes 65552 | tf_op jit(solution)/shard_map/psum | solution.py:59
  151.3 1.7 fusion.47
  153.0 78.0 %psum.15 = f32[16,512]{1,0:T(8,128)S(1)} all-reduce(f32[16,512]{1,0:T(8,128)} %fusion.47), channel_id=1, replica_groups=mesh['group'=8,'sub'=32] {'group','sub'}, use_global_device_ids=true, to_apply=%region_1.0 | all-reduce | flops 8192 | bytes 65536 | tf_op jit(solution)/shard_map/psum | solution.py:68
  231.1 1.9 fusion.58
  233.0 1.4 fusion.57
  234.6 35.0 %all-gather = bf16[32,64,16]{1,2,0:T(8,128)(2,1)} all-gather(bf16[1,64,16]{1,2,0:T(8,128)(2,1)S(1)} %fusion.28), channel_id=1, replica_groups=mesh['group'=8,'sub'=32] {'sub'}, dimensions={0}, use_global_device_ids=true | all-gather | bytes 67584 | tf_op jit(solution)/shard_map/all_gather | solution.py:72
  269.6 1.9 copy.41
  271.5 1.8 gather_fusion
  273.3 2.2 fusion
  275.5 1.0 reshape.101
  276.5 12.7 %collective-permute-start = (f32[16,1,128]{2,1,0:T(1,128)S(1)}, f32[16,1,128]{2,1,0:T(1,128)S(1)}, u32[]{:S(2)}, u32[]{:S(2)}) collective-permute-start(f32[16,1,128]{2,1,0:T(1,128)S(1)} %get-tuple-element.4), channel_id=1, source_target_pairs={{0,32},{32,64},{64,96},{96,128},{128,160},{160,192},{192,224},{1,3... | collective-permute-start | bytes 24584 | tf_op jit(solution)/shard_map/ppermute | solution.py:15
  289.2 1.9 collective-permute-start.1
  291.9 5.6 %all-to-all-start = ((bf16[16,32,128]{2,0,1:T(8,128)(2,1)}), bf16[16,32,128]{2,0,1:T(8,128)(2,1)S(1)}, u32[]{:S(2)}, u32[]{:S(2)}) async-start(bf16[16,32,128]{2,0,1:T(8,128)(2,1)} %copy.36), calls=%async_computation | async-start | bytes 262144 | tf_op jit(solution)/shard_map/all_to_all | solution.py:79
  297.5 1.0 copy.45
  298.6 8.8 %all-to-all-done = bf16[16,32,128]{2,0,1:T(8,128)(2,1)S(1)} async-done(((bf16[16,32,128]{2,0,1:T(8,128)(2,1)}), bf16[16,32,128]{2,0,1:T(8,128)(2,1)S(1)}, u32[]{:S(2)}, u32[]{:S(2)}) %all-to-all-start) | async-done | bytes 131104 | tf_op jit(solution)/shard_map/all_to_all | solution.py:79
  308.2 2.1 fusion.10
  310.4 0.7 broadcast_in_dim_reshape.7
  311.1 0.8 broadcast_in_dim_reshape.6
  (39 shorter events, 2.1 us)
Async XLA Ops:
  7.2 301.0 %copy-start = (bf16[1,8,384,384]{3,2,1,0:T(8,128)(2,1)S(1)}, bf16[1,8,384,384]{3,2,1,0:T(8,128)(2,1)}, u32[]{:S(2)}) copy-start(bf16[1,8,384,384]{3,2,1,0:T(8,128)(2,1)} %param.20) | copy-start | bytes 7077892
  7.2 5.2 %copy-start.2 = (f32[1,16,4352]{2,1,0:T(8,128)S(1)}, f32[1,16,4352]{2,1,0:T(8,128)}, u32[]{:S(2)}) copy-start(f32[1,16,4352]{2,1,0:T(8,128)} %param.13) | copy-start | bytes 835588
  7.2 5.2 %copy-start.4 = (s32[1,128]{1,0:T(1,128)S(1)}, s32[1,128]{1,0:T(1,128)}, u32[]{:S(2)}) copy-start(s32[1,128]{1,0:T(1,128)} %param.17) | copy-start | bytes 1540
  7.2 5.3 %copy-start.5 = (s32[1,8]{1,0:T(1,128)S(1)}, s32[1,8]{1,0:T(1,128)}, u32[]{:S(2)}) copy-start(s32[1,8]{1,0:T(1,128)} %param.18) | copy-start | bytes 100
  7.2 144.1 %all-reduce.3.cloned.1.call-start = ((), (), s32[]{:S(2)}) async-start(), calls=%async_computation.1 | async-start | bytes 131072 | tf_op jit(solution)/shard_map/psum | solution.py:59
  15.3 257.9 %copy-start.1 = (bf16[1,4352,128]{2,1,0:T(8,128)(2,1)S(1)}, bf16[1,4352,128]{2,1,0:T(8,128)(2,1)}, u32[]{:S(2)}) copy-start(bf16[1,4352,128]{2,1,0:T(8,128)(2,1)} %param.22) | copy-start | bytes 3342340
  231.1 3.3 %copy-start.3 = (f32[64,512]{1,0:T(8,128)S(1)}, f32[64,512]{1,0:T(8,128)}, u32[]{:S(2)}) copy-start(f32[64,512]{1,0:T(8,128)} %param.23) | copy-start | bytes 393220
  276.5 22.0 %collective-permute-start = (f32[16,1,128]{2,1,0:T(1,128)S(1)}, f32[16,1,128]{2,1,0:T(1,128)S(1)}, u32[]{:S(2)}, u32[]{:S(2)}) collective-permute-start(f32[16,1,128]{2,1,0:T(1,128)S(1)} %get-tuple-element.4), channel_id=1, source_target_pairs={{0,32},{32,64},{64,96},{96,128},{128,160},{160,192},{192,224},{1,3... | collective-permute-start | bytes 24584 | tf_op jit(solution)/shard_map/ppermute | solution.py:15
  289.2 9.3 %collective-permute-start.1 = (f32[16,1,128]{2,1,0:T(1,128)S(1)}, f32[16,1,128]{2,1,0:T(1,128)S(1)}, u32[]{:S(2)}, u32[]{:S(2)}) collective-permute-start(f32[16,1,128]{2,1,0:T(1,128)S(1)} %get-tuple-element.5), channel_id=1, source_target_pairs={{32,0},{64,32},{96,64},{128,96},{160,128},{192,160},{224,192},{33,... | collective-permute-start | bytes 24584 | tf_op jit(solution)/shard_map/ppermute | solution.py:17
  291.9 15.5 %all-to-all-start = ((bf16[16,32,128]{2,0,1:T(8,128)(2,1)}), bf16[16,32,128]{2,0,1:T(8,128)(2,1)S(1)}, u32[]{:S(2)}, u32[]{:S(2)}) async-start(bf16[16,32,128]{2,0,1:T(8,128)(2,1)} %copy.36), calls=%async_computation | async-start | bytes 262144 | tf_op jit(solution)/shard_map/all_to_all | solution.py:79
Sparse Core Ops, SparseCore 0:
  12.5 138.7 all-reduce.2
where the time goes:
time: 319 us
  waiting for transfers between devices  145 us (45%)
  blocking collectives  113 us (35%)
  starting transfers between devices  20.3 us (6%)
  matrix products  15 us (5%)
  between operations  14.3 us (4%)
  local copies, waits for them, and re-layouts  9.48 us (3%)
    psum x1, waiting for transfers between devices, shards(): level2 = lax.psum(contrib.astype(jnp.bfloat16), 'sub').astype(jnp.float32)  136 us
    psum x1, blocking collectives, shards(): level3 = lax.psum(top_term, ('group', 'sub'))  78 us
    all_gather x1, blocking collectives, shards(): lax.all_gather(coarse2_mine.astype(jnp.bfloat16), 'sub', axis=1, tiled=True)  35 us
    ppermute x1, starting transfers between devices, padded_2(): lax.ppermute(tail, axis, [(i, (i + 1) % count) for i in range(ends)])  12.7 us
    all_to_all x1, waiting for transfers between devices, shards(): lax.all_to_all(slots[:, :nsub, :].astype(jnp.bfloat16), 'sub', split_axis...  8.85 us
  transfers between devices with their start and end apart: 4, of which 2 were waited for; matrix products, arithmetic and copies ran while one was open for 1% of the time, Pallas kernels for 0%

commit v1 on v0

--- a/solution.py
+++ b/solution.py
@@ -69,7 +69,12 @@
     coarse3 = jnp.dot(level3, top_inverse, precision=highest)
     lifted = lax.dot_general(coarse3, group_basis, (((1,), (1,)), ((), ())), precision=highest)
     coarse2_mine = jnp.dot(level2, group_inverse, precision=highest) + lifted
-    coarse2 = lax.all_gather(coarse2_mine.astype(jnp.bfloat16), "sub", axis=1, tiled=True)
+    coarse2 = jnp.concatenate(
+        lax.all_to_all(
+            jnp.stack([coarse2_mine.astype(jnp.bfloat16)] * lax.axis_size("sub")), "sub", 0, 0
+        ),
+        axis=1,
+    )
     values = jnp.take(coarse2, own2[0], axis=1)
     spread = lax.dot_general(
         values, coarse_basis[0], (((1,), (1,)), ((), ())), preferred_element_type=jnp.float32

time: 319 us -> 292 us (0.915)
  blocking collectives: 113 us -> 78 us
  waiting for transfers between devices: 145 us -> 152 us
  local copies, waits for them, and re-layouts: 9.48 us -> 14.5 us
  starting transfers between devices: 20.3 us -> 16.5 us
    all_gather x1 -> x0, blocking collectives: 35 us -> none  [shards(): lax.all_gather(coarse2_mine.astype(jnp.bfloat16), 'sub', axis=1, tiled=True)]
    ppermute x1, starting transfers between devices: 12.7 us -> 4.14 us  [padded_2(): lax.ppermute(tail, axis, [(i, (i + 1) % count) for i in range(ends)])]
    all_to_all x0 -> x1, waiting for transfers between devices: none -> 7.13 us  [shards(): lax.all_to_all(jnp.stack([coarse2_mine.astype(jnp.bfloat16)] * lax.axis_s...]
    all_to_all x0 -> x1, starting transfers between devices: none -> 6.54 us  [shards(): lax.all_to_all(jnp.stack([coarse2_mine.astype(jnp.bfloat16)] * lax.axis_s...]
  transfers between devices with their start and end apart: 4 -> 5, of which waited for: 2 -> 3; matrix products, arithmetic and copies ran while one was open for 1% -> 2% of each run, Pallas kernels for 0% -> 0%
where the time goes in v1:
time: 292 us; the launch traced here: 291 us
  waiting for transfers between devices  152 us (52%)
  blocking collectives  78 us (27%)
  starting transfers between devices  16.5 us (6%)
  local copies, waits for them, and re-layouts  14.5 us (5%)
  matrix products  14.4 us (5%)
  between operations  14.3 us (5%)
    psum x1, waiting for transfers between devices, shards(): level2 = lax.psum(contrib.astype(jnp.bfloat16), 'sub').astype(jnp.float32)  136 us
    psum x1, blocking collectives, shards(): level3 = lax.psum(top_term, ('group', 'sub'))  78 us
    all_to_all x1, waiting for transfers between devices, shards(): lax.all_to_all(slots[:, :nsub, :].astype(jnp.bfloat16), 'sub', split_axis...  8.63 us
    all_to_all x1, waiting for transfers between devices, shards(): lax.all_to_all(jnp.stack([coarse2_mine.astype(jnp.bfloat16)] * lax.axis_s...  7.13 us
    all_to_all x1, starting transfers between devices, shards(): lax.all_to_all(jnp.stack([coarse2_mine.astype(jnp.bfloat16)] * lax.axis_s...  6.54 us
  transfers between devices with their start and end apart: 5, of which 3 were waited for; matrix products, arithmetic and copies ran while one was open for 2% of the time, Pallas kernels for 0%

profile of v1, /device:TPU:1, one launch (start us, length us, event | category | flops | bytes accessed | tf_op | source)
XLA Modules:
  0.0 291.2 jit_solution(15601048837408812498)
XLA Ops:
  7.2 0.8 convert_bitcast_fusion
  8.1 0.8 fusion.44
  8.9 1.6 fusion.25
  10.5 1.8 convolution_convert_fusion
  12.6 2.8 fusion.7
  15.4 135.9 %all-reduce.3.cloned.1.call-done = bf16[16,2048]{1,0:T(8,128)(2,1)} async-done(((bf16[16,2048]{1,0:T(8,128)(2,1)}), bf16[16,2048]{1,0:T(8,128)(2,1)}) %all-reduce.3.cloned.1.call-update) | async-done | bytes 65552 | tf_op jit(solution)/shard_map/psum | solution.py:59
  151.3 1.5 fusion.46
  152.8 78.0 %psum.15 = f32[16,512]{1,0:T(8,128)S(1)} all-reduce(f32[16,512]{1,0:T(8,128)} %fusion.46), channel_id=1, replica_groups=mesh['group'=8,'sub'=32] {'group','sub'}, use_global_device_ids=true, to_apply=%region_1.0 | all-reduce | flops 8192 | bytes 65536 | tf_op jit(solution)/shard_map/psum | solution.py:68
  231.5 1.5 fusion.56
  233.9 1.7 reshape.130
  235.6 6.5 %all-to-all-start = ((bf16[32,2,512]{2,1,0:T(2,128)(2,1)}), bf16[32,2,512]{2,1,0:T(2,128)(2,1)}, u32[]{:S(2)}, u32[]{:S(2)}) async-start(bf16[32,2,512]{2,1,0:T(2,128)(2,1)} %reshape.130), calls=%async_computation | async-start | bytes 131072 | tf_op jit(solution)/shard_map/all_to_all | solution.py:73
  242.1 1.7 copy.39
  243.8 7.1 %all-to-all-done = bf16[32,2,512]{2,1,0:T(2,128)(2,1)} async-done(((bf16[32,2,512]{2,1,0:T(2,128)(2,1)}), bf16[32,2,512]{2,1,0:T(2,128)(2,1)}, u32[]{:S(2)}, u32[]{:S(2)}) %all-to-all-start) | async-done | bytes 65568 | tf_op jit(solution)/shard_map/all_to_all | solution.py:73
  251.0 1.7 reshape.131
  252.6 1.9 copy.33
  254.5 1.8 gather_fusion
  256.3 2.2 fusion
  258.5 1.0 reshape.111
  259.6 4.1 %collective-permute-start = (f32[16,1,128]{2,1,0:T(1,128)S(1)}, f32[16,1,128]{2,1,0:T(1,128)S(1)}, u32[]{:S(2)}, u32[]{:S(2)}) collective-permute-start(f32[16,1,128]{2,1,0:T(1,128)S(1)} %get-tuple-element.4), channel_id=1, source_target_pairs={{0,32},{32,64},{64,96},{96,128},{128,160},{160,192},{192,224},{1,3... | collective-permute-start | bytes 24584 | tf_op jit(solution)/shard_map/ppermute | solution.py:15
  263.7 1.9 collective-permute-start.1
  266.3 3.9 %all-to-all-start.1 = ((bf16[16,32,128]{2,0,1:T(8,128)(2,1)}), bf16[16,32,128]{2,0,1:T(8,128)(2,1)S(1)}, u32[]{:S(2)}, u32[]{:S(2)}) async-start(bf16[16,32,128]{2,0,1:T(8,128)(2,1)} %copy.34), calls=%async_computation.1 | async-start | bytes 262144 | tf_op jit(solution)/shard_map/all_to_all | solution.py:84
  270.2 1.0 copy.41
  271.2 8.6 %all-to-all-done.1 = bf16[16,32,128]{2,0,1:T(8,128)(2,1)S(1)} async-done(((bf16[16,32,128]{2,0,1:T(8,128)(2,1)}), bf16[16,32,128]{2,0,1:T(8,128)(2,1)S(1)}, u32[]{:S(2)}, u32[]{:S(2)}) %all-to-all-start.1) | async-done | bytes 131104 | tf_op jit(solution)/shard_map/all_to_all | solution.py:84
  280.7 2.1 fusion.10
  (51 shorter events, 4.9 us)
Async XLA Ops:
  7.2 273.5 %copy-start = (bf16[1,8,384,384]{3,2,1,0:T(8,128)(2,1)S(1)}, bf16[1,8,384,384]{3,2,1,0:T(8,128)(2,1)}, u32[]{:S(2)}) copy-start(bf16[1,8,384,384]{3,2,1,0:T(8,128)(2,1)} %param.20) | copy-start | bytes 7077892
  7.2 5.2 %copy-start.2 = (f32[1,16,4352]{2,1,0:T(8,128)S(1)}, f32[1,16,4352]{2,1,0:T(8,128)}, u32[]{:S(2)}) copy-start(f32[1,16,4352]{2,1,0:T(8,128)} %param.13) | copy-start | bytes 835588
  7.2 5.2 %copy-start.8 = (s32[1,128]{1,0:T(1,128)S(1)}, s32[1,128]{1,0:T(1,128)}, u32[]{:S(2)}) copy-start(s32[1,128]{1,0:T(1,128)} %param.17) | copy-start | bytes 1540
  7.2 144.1 %all-reduce.3.cloned.1.call-start = ((), (), s32[]{:S(2)}) async-start(), calls=%async_computation.2 | async-start | bytes 131072 | tf_op jit(solution)/shard_map/psum | solution.py:59
  8.9 3.5 %copy-start.6 = (f32[4352]{0:T(1024)}, f32[4352]{0:T(1024)S(1)}, u32[]{:S(2)}) copy-start(f32[4352]{0:T(1024)S(1)} %fusion.44) | copy-start | bytes 52228
  12.5 2.9 %copy-start.9 = (s32[1,8]{1,0:T(1,128)S(1)}, s32[1,8]{1,0:T(1,128)}, u32[]{:S(2)}) copy-start(s32[1,8]{1,0:T(1,128)} %param.18) | copy-start | bytes 100
  12.5 138.8 %copy-start.4 = (f32[64,512]{1,0:T(8,128)S(1)}, f32[64,512]{1,0:T(8,128)}, u32[]{:S(2)}) copy-start(f32[64,512]{1,0:T(8,128)} %param.23) | copy-start | bytes 393220
  12.5 218.3 %copy-start.3 = (f32[512,512]{1,0:T(8,128)S(1)}, f32[512,512]{1,0:T(8,128)}, u32[]{:S(2)}) copy-start(f32[512,512]{1,0:T(8,128)} %param.25) | copy-start | bytes 3145732
  230.9 2.1 copy-start.5
  231.5 24.8 %copy-start.1 = (bf16[1,4352,128]{2,1,0:T(8,128)(2,1)S(1)}, bf16[1,4352,128]{2,1,0:T(8,128)(2,1)}, u32[]{:S(2)}) copy-start(bf16[1,4352,128]{2,1,0:T(8,128)(2,1)} %param.22) | copy-start | bytes 3342340
  231.5 24.8 %copy-start.7 = (f32[4352]{0:T(1024)S(1)}, f32[4352]{0:T(1024)}, u32[]{:S(2)}) copy-start(f32[4352]{0:T(1024)} %copy-done.6) | copy-start | bytes 52228
  235.6 15.4 %all-to-all-start = ((bf16[32,2,512]{2,1,0:T(2,128)(2,1)}), bf16[32,2,512]{2,1,0:T(2,128)(2,1)}, u32[]{:S(2)}, u32[]{:S(2)}) async-start(bf16[32,2,512]{2,1,0:T(2,128)(2,1)} %reshape.130), calls=%async_computation | async-start | bytes 131072 | tf_op jit(solution)/shard_map/all_to_all | solution.py:73
  259.6 11.6 %collective-permute-start = (f32[16,1,128]{2,1,0:T(1,128)S(1)}, f32[16,1,128]{2,1,0:T(1,128)S(1)}, u32[]{:S(2)}, u32[]{:S(2)}) collective-permute-start(f32[16,1,128]{2,1,0:T(1,128)S(1)} %get-tuple-element.4), channel_id=1, source_target_pairs={{0,32},{32,64},{64,96},{96,128},{128,160},{160,192},{192,224},{1,3... | collective-permute-start | bytes 24584 | tf_op jit(solution)/shard_map/ppermute | solution.py:15
  263.7 7.5 %collective-permute-start.1 = (f32[16,1,128]{2,1,0:T(1,128)S(1)}, f32[16,1,128]{2,1,0:T(1,128)S(1)}, u32[]{:S(2)}, u32[]{:S(2)}) collective-permute-start(f32[16,1,128]{2,1,0:T(1,128)S(1)} %get-tuple-element.5), channel_id=1, source_target_pairs={{32,0},{64,32},{96,64},{128,96},{160,128},{192,160},{224,192},{33,... | collective-permute-start | bytes 24584 | tf_op jit(solution)/shard_map/ppermute | solution.py:17
  266.3 13.5 %all-to-all-start.1 = ((bf16[16,32,128]{2,0,1:T(8,128)(2,1)}), bf16[16,32,128]{2,0,1:T(8,128)(2,1)S(1)}, u32[]{:S(2)}, u32[]{:S(2)}) async-start(bf16[16,32,128]{2,0,1:T(8,128)(2,1)} %copy.34), calls=%async_computation.1 | async-start | bytes 262144 | tf_op jit(solution)/shard_map/all_to_all | solution.py:84
Sparse Core Ops, SparseCore 0:
  12.5 138.7 all-reduce.2
